TPU v7x, 32 devices: a whole 2x2x4 slice. The times are simulated.
32 devices in a mesh: ens: 2 (over x), cell: 16 (over z, y, core).
Axes of the slice: x: 2, y: 2, z: 4, core: 2. Of those that a mesh axis runs over, the one named last changes fastest.
Arguments:
- prior_members: float32 [8, 128, 4096], P(None, 'ens', 'cell'), parts along dimension 1, may hold values from -4 to 4
- blocks: bfloat16 [1024, 128, 128], P('cell'), may hold values from -0.3125 to 0.3125
- block_ray: int32 [1024], P('cell'), may hold values from 0 to 15
- block_cell: int32 [1024], P('cell'), may hold values from 0 to 1
- block_count: int32 [16], P('cell'), may hold values from 8 to 64, as said below
- ray_survey: int32 [16], replicated, may hold values from 0 to 7
- observed: float32 [16, 128, 128], P('cell', 'ens'), parts along dimension 1, may hold values from -6 to 6
- noise_scale: float32 [16, 128], P('cell'), may hold values from 0.8 to 1.6
Outputs:
- updated_members: float32 [8, 128, 4096], P(None, 'ens', 'cell'), parts along dimension 1
- last_gradient: bfloat16 [8, 128, 4096], P(None, 'ens', 'cell'), parts along dimension 1
There are 2 independent parts, one for each index of `ens`. A program takes and returns all parts, laid end to end along the dimension named above; an argument that names none is the same for every part. Nothing has to cross between parts.
Inputs may be any that keep to these rules, and one draw needn't show every extreme that they name: `block_count`: slots a slab uses; slots from this count on hold blocks that are not part of the operator. Some slab uses all 64 slots in every draw.
All inputs are finite; a program needn't handle non-finite values.
Results may differ from a plain program's by a relative error of at most 0.0073.
Values may be sent and summed in bfloat16 or wider, within the bound.
No kernel may reach another device: no remote copies, remote signals or barrier semaphores. Data moves between devices by JAX's collectives and lax.ppermute only.
A program may use at most 64 MiB of HBM per device.

v0:
```python
import functools

import jax
import jax.numpy as jnp
from jax import lax
from jax.experimental import pallas as pl
from jax.experimental.pallas import tpu as pltpu
from jax.sharding import PartitionSpec as P

ITERS = 3

ALPHA_PRIOR = 0.5
BETA_TIME = 0.25
GAMMA_DEPTH = 0.25
STEP_SIZE = 0.05
DATA_GAIN = 1.0

SENT_SCALE = 1.0 / 32.0

CHUNK = 8
VMEM_BYTES = 24 * 1024 * 1024
SETUP_VMEM_BYTES = 60 * 1024 * 1024

SMEM = pl.BlockSpec(memory_space=pltpu.SMEM)
VMEM = pl.BlockSpec(memory_space=pltpu.VMEM)
ANY = pl.BlockSpec(memory_space=pl.ANY)
HBM = pl.BlockSpec(memory_space=pltpu.HBM)


class Order:
    def __init__(self, count, ray_blocks):
        self.owned = ray_blocks // count
        self.half_blocks = ray_blocks // 2

    def core(self):
        return lax.rem(lax.axis_index("cell"), 2)

    def place(self, core, q):
        owner = lax.div(q, self.owned)
        other_core = lax.rem(owner + core, 2)
        first = other_core * self.half_blocks + lax.div(owner, 2) * self.owned
        return first + lax.rem(q, self.owned)

    def survey(self, core, survey_ref, i):
        other_core, rest = divmod(i, self.half_blocks)
        chip, offset = divmod(rest, self.owned)
        owner = 2 * chip + (1 - core if other_core else core)
        return survey_ref[owner * self.owned + offset]


def forward(order, survey_ref, half_ref, dense_ref, own_ref, away_ref):
    core = order.core()
    half = own_ref.shape[0]
    for i in range(2 * half):
        travel = lax.dot_general(
            half_ref[order.survey(core, survey_ref, i)],
            dense_ref[i],
            (((1,), (1,)), ((), ())),
            preferred_element_type=jnp.float32,
        )
        if i < half:
            own_ref[i] = travel
        else:
            away_ref[i - half] = travel


def setup_kernel(
    order, count_ref, ray_hbm, cell_hbm, survey_hbm, members_hbm, blocks_hbm,
    dense_ref, half_ref, own_ref, away_ref,
    ray_ref, cell_ref, survey_ref, members_ref, staged, upper, lower, small_sems, sems,
):
    slots, rays, width = blocks_hbm.shape
    chunks = slots // CHUNK
    core = order.core()
    small = [
        pltpu.make_async_copy(source, target, small_sems.at[i])
        for i, (source, target) in enumerate(
            (
                (ray_hbm, ray_ref),
                (cell_hbm, cell_ref),
                (survey_hbm, survey_ref),
                (members_hbm, members_ref),
            )
        )
    ]
    large = []
    for i in range(chunks):
        part = pl.ds(i * CHUNK, CHUNK)
        large.append(pltpu.make_async_copy(blocks_hbm.at[part], staged.at[part], sems.at[i]))
    for copy in small + large:
        copy.start()
    upper[...] = jnp.zeros_like(upper)
    lower[...] = jnp.zeros_like(lower)
    middle = rays // 2
    for copy in small:
        copy.wait()
    half_ref[...] = members_ref[...].astype(half_ref.dtype)
    count = count_ref[0]
    spare = dense_ref.shape[0]
    for i in range(chunks):
        large[i].wait()
        for k in range(i * CHUNK, (i + 1) * CHUNK):
            place = jnp.where(k < count, order.place(core, ray_ref[k]), spare)
            b = cell_ref[k]
            upper[b, place] = upper[b, place] + staged[k, :middle].astype(jnp.float32)
            lower[b, place] = lower[b, place] + staged[k, middle:].astype(jnp.float32)
    for b in range(upper.shape[0]):
        cells = slice(b * width, (b + 1) * width)
        dense_ref[:, :middle, cells] = upper[b, :spare].astype(dense_ref.dtype)
        dense_ref[:, middle:, cells] = lower[b, :spare].astype(dense_ref.dtype)
    forward(order, survey_ref, half_ref, dense_ref, own_ref, away_ref)


def misfit_kernel(travel_ref, observed_ref, noise_ref, token_ref, out_ref):
    del token_ref
    travel = travel_ref[...]
    spread = noise_ref[...][:, None, :]
    scaled = (travel - observed_ref[...]) / spread
    residual = DATA_GAIN * scaled / (spread * (1.0 + scaled * scaled))
    out_ref[...] = jnp.broadcast_to(residual.astype(out_ref.dtype)[None], out_ref.shape)


def arrival_kernel(observed_ref, halo_ref, token_ref):
    del observed_ref, halo_ref
    token_ref[...] = jnp.zeros_like(token_ref)


def add_products(order, survey_ref, low, products, upper, lower):
    core = order.core()
    middle = upper.shape[1]
    for i, product in enumerate(products):
        s = order.survey(core, survey_ref, low + i)
        upper[s] = upper[s] + product[:middle]
        lower[s] = lower[s] + product[middle:]


def gradient_kernel(
    order, survey_ref, residual_ref, dense_ref, members_ref, prior_ref, chip_ref, link_ref,
    upper, lower,
):
    products = [
        jnp.dot(residual_ref[i], dense_ref[i], preferred_element_type=jnp.float32)
        for i in range(residual_ref.shape[0])
    ]
    surveys = members_ref.shape[0]
    middle = upper.shape[1]
    for s in range(surveys):
        m = members_ref[s]
        value = ALPHA_PRIOR * (m - prior_ref[s])
        if s > 0:
            value = value + BETA_TIME * (m - members_ref[s - 1])
        if s < surveys - 1:
            value = value + BETA_TIME * (m - members_ref[s + 1])
        neighbours = chip_ref[s].astype(jnp.float32) + link_ref[s].astype(jnp.float32)
        value = value + GAMMA_DEPTH * (2.0 * m - neighbours)
        upper[s] = value[:middle]
        lower[s] = value[middle:]
    add_products(order, survey_ref, 0, products, upper, lower)


def finish_gradient(
    order, survey_ref, residual_ref, dense_ref, upper_ref, lower_ref, upper, lower
):
    half = residual_ref.shape[0]
    products = [
        jnp.dot(residual_ref[i], dense_ref[half + i], preferred_element_type=jnp.float32)
        for i in range(half)
    ]
    upper[...] = upper_ref[...]
    lower[...] = lower_ref[...]
    add_products(order, survey_ref, half, products, upper, lower)


def step_kernel(
    order, survey_ref, residual_ref, dense_ref, upper_ref, lower_ref, members_ref,
    out_ref, half_ref, own_ref, away_ref,
    upper, lower,
):
    finish_gradient(order, survey_ref, residual_ref, dense_ref, upper_ref, lower_ref, upper, lower)
    middle = upper.shape[1]
    for rows, grad in ((slice(0, middle), upper), (slice(middle, None), lower)):
        updated = members_ref[:, rows] - STEP_SIZE * grad[...]
        out_ref[:, rows] = updated
        half_ref[:, rows] = updated.astype(half_ref.dtype)
    forward(order, survey_ref, half_ref, dense_ref, own_ref, away_ref)


def last_kernel(
    order, survey_ref, residual_ref, dense_ref, upper_ref, lower_ref, members_ref,
    out_ref, gradient_ref,
    upper, lower,
):
    finish_gradient(order, survey_ref, residual_ref, dense_ref, upper_ref, lower_ref, upper, lower)
    middle = upper.shape[1]
    for rows, grad in ((slice(0, middle), upper), (slice(middle, None), lower)):
        out_ref[:, rows] = members_ref[:, rows] - STEP_SIZE * grad[...]
        gradient_ref[:, rows] = grad[...].astype(gradient_ref.dtype)


def shards(
    prior_members, blocks, block_ray, block_cell, block_count, ray_survey, observed, noise_scale
):
    surveys, ensemble, cells_dev = prior_members.shape
    slots, rays, width = blocks.shape
    ray_blocks = ray_survey.shape[0]
    count = lax.axis_size("cell")
    order = Order(count, ray_blocks)
    owned, half_blocks = order.owned, order.half_blocks
    chips = count // 2
    params = pltpu.CompilerParams(vmem_limit_bytes=VMEM_BYTES)

    def bf16(*shape):
        return jax.ShapeDtypeStruct(shape, jnp.bfloat16)

    def f32(*shape):
        return jax.ShapeDtypeStruct(shape, jnp.float32)

    members_f32 = f32(surveys, ensemble, cells_dev)
    part_f32 = f32(surveys, ensemble // 2, cells_dev)
    members_bf16 = bf16(surveys, ensemble, cells_dev)
    travels = (f32(half_blocks, ensemble, rays),) * 2

    in_hbm = [
        pltpu.with_memory_space_constraint(array, pltpu.HBM)
        for array in (block_ray, block_cell, ray_survey, prior_members, blocks)
    ]
    dense, half, own, away = pl.pallas_call(
        functools.partial(setup_kernel, order),
        out_shape=(bf16(ray_blocks, rays, cells_dev), members_bf16) + travels,
        in_specs=[SMEM] + [HBM] * 5,
        out_specs=(VMEM,) * 4,
        scratch_shapes=[
            pltpu.SMEM(block_ray.shape, jnp.int32),
            pltpu.SMEM(block_cell.shape, jnp.int32),
            pltpu.SMEM(ray_survey.shape, jnp.int32),
            pltpu.VMEM(prior_members.shape, jnp.float32),
            pltpu.VMEM(blocks.shape, blocks.dtype),
            pltpu.VMEM((cells_dev // width, ray_blocks + 1, rays // 2, width), jnp.float32),
            pltpu.VMEM((cells_dev // width, ray_blocks + 1, rays // 2, width), jnp.float32),
            pltpu.SemaphoreType.DMA((4,)),
            pltpu.SemaphoreType.DMA((slots // CHUNK,)),
        ],
        compiler_params=pltpu.CompilerParams(vmem_limit_bytes=VMEM_BYTES),
    )(block_count, *in_hbm)

    chip_pairs = [(i, i ^ 1) for i in range(count)]
    link_pairs = [pair for i in range(1, count - 1, 2) for pair in ((i, i + 1), (i + 1, i))]
    same_core = [list(range(core, count, 2)) for core in range(2)]

    def exchange(array):
        return lax.all_to_all(
            array, "cell", split_axis=0, concat_axis=0, axis_index_groups=same_core, tiled=True
        )

    members = prior_members
    for iteration in range(ITERS):
        received = lax.ppermute(away, "cell", chip_pairs)
        chip_halo = lax.ppermute(half, "cell", chip_pairs)
        received, chip_halo = lax.optimization_barrier((received, chip_halo))
        chip_travel = ((own + received) * SENT_SCALE).astype(jnp.float16)
        link_halo = lax.ppermute(half, "cell", link_pairs)
        parts = exchange(chip_travel)
        parts, after_parts = lax.optimization_barrier((parts, observed))
        token = pl.pallas_call(
            arrival_kernel,
            out_shape=f32(8, 128),
            in_specs=[ANY] * 2,
            out_specs=VMEM,
            compiler_params=params,
        )(after_parts, link_halo)
        parts, token = lax.optimization_barrier((parts, token))
        parts = parts.reshape(chips, owned, ensemble, rays).astype(jnp.float32)
        travel = jnp.sum(parts, axis=0) / SENT_SCALE
        copies = pl.pallas_call(
            misfit_kernel,
            out_shape=bf16(chips, owned, ensemble, rays),
            in_specs=[VMEM] * 3 + [ANY],
            out_specs=VMEM,
            compiler_params=params,
        )(travel, observed, noise_scale, token)
        residual = exchange(copies.reshape(half_blocks, ensemble, rays))
        other_residual = lax.ppermute(residual, "cell", chip_pairs)
        partial = pl.pallas_call(
            functools.partial(gradient_kernel, order),
            out_shape=(part_f32, part_f32),
            in_specs=[SMEM] + [VMEM] * 6,
            out_specs=(VMEM, VMEM),
            compiler_params=params,
        )(ray_survey, residual, dense, members, prior_members, chip_halo, link_halo)
        last = iteration == ITERS - 1
        outputs = (members_f32, members_bf16) + (() if last else travels)
        results = pl.pallas_call(
            functools.partial(last_kernel if last else step_kernel, order),
            out_shape=outputs,
            in_specs=[SMEM] + [VMEM] * 5,
            out_specs=(VMEM,) * len(outputs),
            scratch_shapes=[pltpu.VMEM(part_f32.shape, jnp.float32)] * 2,
            compiler_params=params,
        )(ray_survey, other_residual, dense, *partial, members)
        if last:
            return results
        members, half, own, away = results


def solution(mesh):
    placed = (
        P(None, "ens", "cell"),
        P("cell", None, None),
        P("cell"),
        P("cell"),
        P("cell"),
        P(),
        P("cell", "ens", None),
        P("cell", None),
    )
    return jax.shard_map(
        shards,
        mesh=mesh,
        in_specs=placed,
        out_specs=(P(None, "ens", "cell"), P(None, "ens", "cell")),
        check_vma=False,
    )
```

profile of v0, /device:TPU:0, one launch (start us, length us, event | category | flops | bytes accessed | tf_op | source)
XLA Modules:
  0.0 85.7 jit_solution(11884329681297000005)
XLA Ops:
  1.3 2.8 %shard_map.95 = (bf16[16,128,256]{2,1,0:T(8,128)(2,1)S(1)}, bf16[8,64,256]{2,1,0:T(8,128)(2,1)S(1)}, f32[8,64,128]{2,1,0:T(8,128)S(1)}, f32[8,64,128]{2,1,0:T(8,128)S(1)}) custom-call(s32[1]{0:T(128)S(6)} %copy.10.count_ref, s32[64]{0:T(128)} %ray_hbm.1, s32[64]{0:T(128)} %cell_hbm.1, s32[16]{0:T(128)} %survey_ref.11, f32[8,64,256]{2,1,0:T(8,128)} %prior_ref.5, ...), custom_call_target="tpu_custom_call" | custom-call | tf_op jit(solution)/shard_map/pallas_call | solution.py:227
  4.2 0.5 collective-permute-start
  4.7 0.1 collective-permute-start.1
  4.8 0.7 collective-permute-start.2
  5.5 0.4 collective-permute-done
  5.9 0.4 collective-permute-done.1.chip_ref
  6.3 15.4 %all_to_all.30 = f16[8,64,128]{2,1,0:T(8,128)(2,1)S(1)} all-to-all(f16[8,64,128]{2,1,0:T(8,128)(2,1)S(1)} %multiply_convert_fusion.2), channel_id=1, replica_groups={{0,2,4,6,8,10,12,14},{1,3,5,7,9,11,13,15},{16,18,20,22,24,26,28,30},{17..., dimensions={0} | all-to-all | bytes 262144 | tf_op jit(solution)/shard_map/all_to_all | solution.py:251
  21.6 0.0 collective-permute-done.2.halo_ref.link_ref
  21.7 9.9 %all_to_all.31.residual_ref = bf16[8,64,128]{2,1,0:T(8,128)(2,1)S(1)} all-to-all(bf16[8,64,128]{2,1,0:T(8,128)(2,1)S(1)} %bitcast.9), channel_id=1, replica_groups={{0,2,4,6,8,10,12,14},{1,3,5,7,9,11,13,15},{16,18,20,22,24,26,28,30},{17..., dimensions={0} | all-to-all | bytes 262144 | tf_op jit(solution)/shard_map/all_to_all | solution.py:251
  31.6 0.9 %shard_map.98 = (f32[8,32,256]{2,1,0:T(8,128)S(1)}, f32[8,32,256]{2,1,0:T(8,128)S(1)}) custom-call(s32[16]{0:T(128)S(1)} %copy-done.2, bf16[8,64,128]{2,1,0:T(8,128)(2,1)S(1)} %all_to_all.31.residual_ref, bf16[16,128,256]{2,1,0:T(8,128)(2,1)S(1)} %get-tuple-element.46.dense_ref, f32[8,64,256]{2,1,0:T(8,128)S(1)} %copy-done, f32[8,64,256]{2,1,0:T(8,128)S(1)} %copy-done, ...), custom_call_target="tpu_custom_call" | custom-call | tf_op jit(solution)/shard_map/pallas_call | solution.py:283
  32.5 0.4 collective-permute-done.3.residual_ref
  32.9 1.3 %shard_map.99 = (f32[8,64,256]{2,1,0:T(8,128)S(1)}, bf16[8,64,256]{2,1,0:T(8,128)(2,1)S(1)}, f32[8,64,128]{2,1,0:T(8,128)S(1)}, f32[8,64,128]{2,1,0:T(8,128)S(1)}) custom-call(s32[16]{0:T(128)S(1)} %copy-done.2, bf16[8,64,128]{2,1,0:T(8,128)(2,1)S(1)} %collective-permute-done.3.residual_ref, bf16[16,128,256]{2,1,0:T(8,128)(2,1)S(1)} %get-tuple-element.46.dense_ref, ...), custom_call_target="tpu_custom_call" | custom-call | tf_op jit(solution)/shard_map/pallas_call | solution.py:292
  34.3 0.2 collective-permute-start.4
  34.5 0.4 collective-permute-start.5
  34.8 0.7 collective-permute-start.6
  35.5 0.4 collective-permute-done.4
  35.9 0.4 collective-permute-done.5.chip_ref
  36.3 10.9 %all_to_all.32 = f16[8,64,128]{2,1,0:T(8,128)(2,1)S(1)} all-to-all(f16[8,64,128]{2,1,0:T(8,128)(2,1)S(1)} %multiply_convert_fusion.1), channel_id=1, replica_groups={{0,2,4,6,8,10,12,14},{1,3,5,7,9,11,13,15},{16,18,20,22,24,26,28,30},{17..., dimensions={0} | all-to-all | bytes 262144 | tf_op jit(solution)/shard_map/all_to_all | solution.py:251
  47.3 9.8 %all_to_all.33.residual_ref = bf16[8,64,128]{2,1,0:T(8,128)(2,1)S(1)} all-to-all(bf16[8,64,128]{2,1,0:T(8,128)(2,1)S(1)} %bitcast.10), channel_id=1, replica_groups={{0,2,4,6,8,10,12,14},{1,3,5,7,9,11,13,15},{16,18,20,22,24,26,28,30},{17..., dimensions={0} | all-to-all | bytes 262144 | tf_op jit(solution)/shard_map/all_to_all | solution.py:251
  57.1 0.9 %shard_map.102 = (f32[8,32,256]{2,1,0:T(8,128)S(1)}, f32[8,32,256]{2,1,0:T(8,128)S(1)}) custom-call(s32[16]{0:T(128)S(1)} %copy-done.2, bf16[8,64,128]{2,1,0:T(8,128)(2,1)S(1)} %all_to_all.33.residual_ref, bf16[16,128,256]{2,1,0:T(8,128)(2,1)S(1)} %get-tuple-element.46.dense_ref, f32[8,64,256]{2,1,0:T(8,128)S(1)} %get-tuple-element.58.members_ref, ...), custom_call_target="tpu_custom_call" | custom-call | tf_op jit(solution)/shard_map/pallas_call | solution.py:283
  58.0 0.4 collective-permute-done.7.residual_ref
  58.4 1.3 %shard_map.103 = (f32[8,64,256]{2,1,0:T(8,128)S(1)}, bf16[8,64,256]{2,1,0:T(8,128)(2,1)S(1)}, f32[8,64,128]{2,1,0:T(8,128)S(1)}, f32[8,64,128]{2,1,0:T(8,128)S(1)}) custom-call(s32[16]{0:T(128)S(1)} %copy-done.2, bf16[8,64,128]{2,1,0:T(8,128)(2,1)S(1)} %collective-permute-done.7.residual_ref, bf16[16,128,256]{2,1,0:T(8,128)(2,1)S(1)} %get-tuple-element.46.dense_ref, ...), custom_call_target="tpu_custom_call" | custom-call | tf_op jit(solution)/shard_map/pallas_call | solution.py:292
  59.8 0.2 collective-permute-start.8
  60.0 0.4 collective-permute-start.9
  60.3 0.7 collective-permute-start.10
  61.0 0.4 collective-permute-done.8
  61.4 0.4 collective-permute-done.9.chip_ref
  61.8 10.9 %all_to_all.34 = f16[8,64,128]{2,1,0:T(8,128)(2,1)S(1)} all-to-all(f16[8,64,128]{2,1,0:T(8,128)(2,1)S(1)} %multiply_convert_fusion), channel_id=1, replica_groups={{0,2,4,6,8,10,12,14},{1,3,5,7,9,11,13,15},{16,18,20,22,24,26,28,30},{17..., dimensions={0} | all-to-all | bytes 262144 | tf_op jit(solution)/shard_map/all_to_all | solution.py:251
  72.8 9.8 %all_to_all.35.residual_ref = bf16[8,64,128]{2,1,0:T(8,128)(2,1)S(1)} all-to-all(bf16[8,64,128]{2,1,0:T(8,128)(2,1)S(1)} %bitcast.11), channel_id=1, replica_groups={{0,2,4,6,8,10,12,14},{1,3,5,7,9,11,13,15},{16,18,20,22,24,26,28,30},{17..., dimensions={0} | all-to-all | bytes 262144 | tf_op jit(solution)/shard_map/all_to_all | solution.py:251
  82.6 0.9 %shard_map.106 = (f32[8,32,256]{2,1,0:T(8,128)S(1)}, f32[8,32,256]{2,1,0:T(8,128)S(1)}) custom-call(s32[16]{0:T(128)S(1)} %copy-done.2, bf16[8,64,128]{2,1,0:T(8,128)(2,1)S(1)} %all_to_all.35.residual_ref, bf16[16,128,256]{2,1,0:T(8,128)(2,1)S(1)} %get-tuple-element.46.dense_ref, f32[8,64,256]{2,1,0:T(8,128)S(1)} %get-tuple-element.70.members_ref, ...), custom_call_target="tpu_custom_call" | custom-call | tf_op jit(solution)/shard_map/pallas_call | solution.py:283
  83.5 0.4 collective-permute-done.11.residual_ref
  83.9 1.7 %shard_map.107 = (f32[8,64,256]{2,1,0:T(8,128)}, bf16[8,64,256]{2,1,0:T(8,128)(2,1)}) custom-call(s32[16]{0:T(128)S(1)} %copy-done.2, bf16[8,64,128]{2,1,0:T(8,128)(2,1)S(1)} %collective-permute-done.11.residual_ref, bf16[16,128,256]{2,1,0:T(8,128)(2,1)S(1)} %get-tuple-element.46.dense_ref, f32[8,32,256]{2,1,0:T(8,128)S(1)} %get-tuple-element.72.upper_ref, ...), custom_call_target="tpu_custom_call" | custom-call | tf_op jit(solution)/shard_map/pallas_call | solution.py:292
  (28 shorter events, 0.3 us)
Async XLA Ops:
  0.6 21.0 %copy-start.1 = (f32[1,64,128]{2,1,0:T(8,128)S(1)}, f32[1,64,128]{2,1,0:T(8,128)}, u32[]{:S(2)}) copy-start(f32[1,64,128]{2,1,0:T(8,128)} %observed_ref.8) | copy-start | bytes 98308
  0.6 21.1 %copy-start.3 = (f32[1,128]{1,0:T(1,128)S(1)}, f32[1,128]{1,0:T(1,128)}, u32[]{:S(2)}) copy-start(f32[1,128]{1,0:T(1,128)} %noise_ref.5) | copy-start | bytes 1540
  1.3 30.3 %copy-start = (f32[8,64,256]{2,1,0:T(8,128)S(1)}, f32[8,64,256]{2,1,0:T(8,128)}, u32[]{:S(2)}) copy-start(f32[8,64,256]{2,1,0:T(8,128)} %prior_ref.5) | copy-start | bytes 1572868
  1.3 30.3 %copy-start.2 = (s32[16]{0:T(128)S(1)}, s32[16]{0:T(128)}, u32[]{:S(2)}) copy-start(s32[16]{0:T(128)} %survey_ref.11) | copy-start | bytes 196
  4.2 1.7 %collective-permute-start = (f32[8,64,128]{2,1,0:T(8,128)S(1)}, f32[8,64,128]{2,1,0:T(8,128)S(1)}, u32[]{:S(2)}, u32[]{:S(2)}) collective-permute-start(f32[8,64,128]{2,1,0:T(8,128)S(1)} %get-tuple-element.39), channel_id=1, source_target_pairs={{0,1},{1,0},{2,3},{3,2},{4,5},{5,4},{6,7},{7,6},{8,9},{9,8},{10,11... | collective-permute-start | bytes 786440 | tf_op jit(solution)/shard_map/ppermute | solution.py:257
  4.7 1.5 %collective-permute-start.1 = (bf16[8,64,256]{2,1,0:T(8,128)(2,1)S(1)}, bf16[8,64,256]{2,1,0:T(8,128)(2,1)S(1)}, u32[]{:S(2)}, u32[]{:S(2)}) collective-permute-start(bf16[8,64,256]{2,1,0:T(8,128)(2,1)S(1)} %get-tuple-element.40), channel_id=1, source_target_pairs={{0,1},{1,0},{2,3},{3,2},{4,5},{5,4},{6,7},{7,6},{8,9},{9,8},{10,11... | collective-permute-start | bytes 786440 | tf_op jit(solution)/shard_map/ppermute | solution.py:258
  4.8 16.9 %collective-permute-start.2 = (bf16[8,64,256]{2,1,0:T(8,128)(2,1)S(1)}, bf16[8,64,256]{2,1,0:T(8,128)(2,1)S(1)}, u32[]{:S(2)}, u32[]{:S(2)}) collective-permute-start(bf16[8,64,256]{2,1,0:T(8,128)(2,1)S(1)} %get-tuple-element.40), channel_id=1, source_target_pairs={{1,2},{2,1},{3,4},{4,3},{5,6},{6,5},{7,8},{8,7},{9,10},{10,9},{11,... | collective-permute-start | bytes 786440 | tf_op jit(solution)/shard_map/ppermute | solution.py:261
  31.6 1.3 %collective-permute-start.3 = (bf16[8,64,128]{2,1,0:T(8,128)(2,1)S(1)}, bf16[8,64,128]{2,1,0:T(8,128)(2,1)S(1)}, u32[]{:S(2)}, u32[]{:S(2)}) collective-permute-start(bf16[8,64,128]{2,1,0:T(8,128)(2,1)S(1)} %all_to_all.31.residual_ref), channel_id=1, source_target_pairs={{0,1},{1,0},{2,3},{3,2},{4,5},{5,4},{6,7},{7,6},{8,9},{9,8},{10,11... | collective-permute-start | bytes 393224 | tf_op jit(solution)/shard_map/ppermute | solution.py:282
  34.3 1.6 %collective-permute-start.4 = (f32[8,64,128]{2,1,0:T(8,128)S(1)}, f32[8,64,128]{2,1,0:T(8,128)S(1)}, u32[]{:S(2)}, u32[]{:S(2)}) collective-permute-start(f32[8,64,128]{2,1,0:T(8,128)S(1)} %get-tuple-element.51), channel_id=1, source_target_pairs={{0,1},{1,0},{2,3},{3,2},{4,5},{5,4},{6,7},{7,6},{8,9},{9,8},{10,11... | collective-permute-start | bytes 786440 | tf_op jit(solution)/shard_map/ppermute | solution.py:257
  34.5 1.8 %collective-permute-start.5 = (bf16[8,64,256]{2,1,0:T(8,128)(2,1)S(1)}, bf16[8,64,256]{2,1,0:T(8,128)(2,1)S(1)}, u32[]{:S(2)}, u32[]{:S(2)}) collective-permute-start(bf16[8,64,256]{2,1,0:T(8,128)(2,1)S(1)} %get-tuple-element.52), channel_id=1, source_target_pairs={{0,1},{1,0},{2,3},{3,2},{4,5},{5,4},{6,7},{7,6},{8,9},{9,8},{10,11... | collective-permute-start | bytes 786440 | tf_op jit(solution)/shard_map/ppermute | solution.py:258
  34.8 12.3 %collective-permute-start.6 = (bf16[8,64,256]{2,1,0:T(8,128)(2,1)S(1)}, bf16[8,64,256]{2,1,0:T(8,128)(2,1)S(1)}, u32[]{:S(2)}, u32[]{:S(2)}) collective-permute-start(bf16[8,64,256]{2,1,0:T(8,128)(2,1)S(1)} %get-tuple-element.52), channel_id=1, source_target_pairs={{1,2},{2,1},{3,4},{4,3},{5,6},{6,5},{7,8},{8,7},{9,10},{10,9},{11,... | collective-permute-start | bytes 786440 | tf_op jit(solution)/shard_map/ppermute | solution.py:261
  57.1 1.3 %collective-permute-start.7 = (bf16[8,64,128]{2,1,0:T(8,128)(2,1)S(1)}, bf16[8,64,128]{2,1,0:T(8,128)(2,1)S(1)}, u32[]{:S(2)}, u32[]{:S(2)}) collective-permute-start(bf16[8,64,128]{2,1,0:T(8,128)(2,1)S(1)} %all_to_all.33.residual_ref), channel_id=1, source_target_pairs={{0,1},{1,0},{2,3},{3,2},{4,5},{5,4},{6,7},{7,6},{8,9},{9,8},{10,11... | collective-permute-start | bytes 393224 | tf_op jit(solution)/shard_map/ppermute | solution.py:282
  59.8 1.6 %collective-permute-start.8 = (f32[8,64,128]{2,1,0:T(8,128)S(1)}, f32[8,64,128]{2,1,0:T(8,128)S(1)}, u32[]{:S(2)}, u32[]{:S(2)}) collective-permute-start(f32[8,64,128]{2,1,0:T(8,128)S(1)} %get-tuple-element.63), channel_id=1, source_target_pairs={{0,1},{1,0},{2,3},{3,2},{4,5},{5,4},{6,7},{7,6},{8,9},{9,8},{10,11... | collective-permute-start | bytes 786440 | tf_op jit(solution)/shard_map/ppermute | solution.py:257
  60.0 1.8 %collective-permute-start.9 = (bf16[8,64,256]{2,1,0:T(8,128)(2,1)S(1)}, bf16[8,64,256]{2,1,0:T(8,128)(2,1)S(1)}, u32[]{:S(2)}, u32[]{:S(2)}) collective-permute-start(bf16[8,64,256]{2,1,0:T(8,128)(2,1)S(1)} %get-tuple-element.64), channel_id=1, source_target_pairs={{0,1},{1,0},{2,3},{3,2},{4,5},{5,4},{6,7},{7,6},{8,9},{9,8},{10,11... | collective-permute-start | bytes 786440 | tf_op jit(solution)/shard_map/ppermute | solution.py:258
  60.3 12.3 %collective-permute-start.10 = (bf16[8,64,256]{2,1,0:T(8,128)(2,1)S(1)}, bf16[8,64,256]{2,1,0:T(8,128)(2,1)S(1)}, u32[]{:S(2)}, u32[]{:S(2)}) collective-permute-start(bf16[8,64,256]{2,1,0:T(8,128)(2,1)S(1)} %get-tuple-element.64), channel_id=1, source_target_pairs={{1,2},{2,1},{3,4},{4,3},{5,6},{6,5},{7,8},{8,7},{9,10},{10,9},{11,... | collective-permute-start | bytes 786440 | tf_op jit(solution)/shard_map/ppermute | solution.py:261
  82.6 1.3 %collective-permute-start.11 = (bf16[8,64,128]{2,1,0:T(8,128)(2,1)S(1)}, bf16[8,64,128]{2,1,0:T(8,128)(2,1)S(1)}, u32[]{:S(2)}, u32[]{:S(2)}) collective-permute-start(bf16[8,64,128]{2,1,0:T(8,128)(2,1)S(1)} %all_to_all.35.residual_ref), channel_id=1, source_target_pairs={{0,1},{1,0},{2,3},{3,2},{4,5},{5,4},{6,7},{7,6},{8,9},{9,8},{10,11... | collective-permute-start | bytes 393224 | tf_op jit(solution)/shard_map/ppermute | solution.py:282
where the time goes:
time: 86.1 us; the launch traced here: 85.7 us
  blocking collectives  66.7 us (77%)
  Pallas kernels  10 us (12%)
  starting transfers between devices  3.74 us (4%)
  waiting for transfers between devices  3.47 us (4%)
  between operations  1.49 us (2%)
    all_to_all x6, blocking collectives, exchange(): lax.all_to_all(array, 'cell', split_axis=0, concat_axis=0, axis_index_gro...  66.7 us
    pallas_call x3, Pallas kernels, shards(): pl.pallas_call(functools.partial(last_kernel if last else step_kernel, or...  4.33 us
    pallas_call x1, Pallas kernels, shards(): pl.pallas_call(functools.partial(setup_kernel, order), out_shape=(bf16(ra...  2.84 us
    pallas_call x3, Pallas kernels, shards(): pl.pallas_call(functools.partial(gradient_kernel, order), out_shape=(part...  2.78 us
    ppermute x3, starting transfers between devices, shards(): link_halo = lax.ppermute(half, 'cell', link_pairs)  2 us
  transfers between devices with their start and end apart: 12, of which 9 were waited for; matrix products, arithmetic and copies ran while one was open for 0% of the time, Pallas kernels for 3%

commit v1 on v0

--- a/solution.py
+++ b/solution.py
@@ -87,14 +87,13 @@
     for i in range(chunks):
         part = pl.ds(i * CHUNK, CHUNK)
         large.append(pltpu.make_async_copy(blocks_hbm.at[part], staged.at[part], sems.at[i]))
-    for copy in small + large:
+    for copy in small[:-1] + large + small[-1:]:
         copy.start()
     upper[...] = jnp.zeros_like(upper)
     lower[...] = jnp.zeros_like(lower)
     middle = rays // 2
-    for copy in small:
+    for copy in small[:-1]:
         copy.wait()
-    half_ref[...] = members_ref[...].astype(half_ref.dtype)
     count = count_ref[0]
     spare = dense_ref.shape[0]
     for i in range(chunks):
@@ -108,6 +107,8 @@
         cells = slice(b * width, (b + 1) * width)
         dense_ref[:, :middle, cells] = upper[b, :spare].astype(dense_ref.dtype)
         dense_ref[:, middle:, cells] = lower[b, :spare].astype(dense_ref.dtype)
+    small[-1].wait()
+    half_ref[...] = members_ref[...].astype(half_ref.dtype)
     forward(order, survey_ref, half_ref, dense_ref, own_ref, away_ref)
 
 

time: 86.1 us -> 85.6 us (level)
  no operation moved by 1% of the time
where the time goes in v1:
time: 85.6 us; the launch traced here: 85.2 us
  blocking collectives  66.7 us (78%)
  Pallas kernels  9.55 us (11%)
  starting transfers between devices  3.74 us (4%)
  waiting for transfers between devices  3.47 us (4%)
  between operations  1.48 us (2%)
    all_to_all x6, blocking collectives, exchange(): lax.all_to_all(array, 'cell', split_axis=0, concat_axis=0, axis_index_gro...  66.7 us
    pallas_call x3, Pallas kernels, shards(): pl.pallas_call(functools.partial(last_kernel if last else step_kernel, or...  4.34 us
    pallas_call x3, Pallas kernels, shards(): pl.pallas_call(functools.partial(gradient_kernel, order), out_shape=(part...  2.78 us
    pallas_call x1, Pallas kernels, shards(): pl.pallas_call(functools.partial(setup_kernel, order), out_shape=(bf16(ra...  2.34 us
    ppermute x3, starting transfers between devices, shards(): link_halo = lax.ppermute(half, 'cell', link_pairs)  2 us
  transfers between devices with their start and end apart: 12, of which 9 were waited for; matrix products, arithmetic and copies ran while one was open for 0% of the time, Pallas kernels for 3%

profile of v1, /device:TPU:0, one launch (start us, length us, event | category | flops | bytes accessed | tf_op | source)
XLA Modules:
  0.0 85.2 jit_solution(6402035860922349251)
XLA Ops:
  1.3 2.3 %shard_map.95 = (bf16[16,128,256]{2,1,0:T(8,128)(2,1)S(1)}, bf16[8,64,256]{2,1,0:T(8,128)(2,1)S(1)}, f32[8,64,128]{2,1,0:T(8,128)S(1)}, f32[8,64,128]{2,1,0:T(8,128)S(1)}) custom-call(s32[1]{0:T(128)S(6)} %copy.10.count_ref, s32[64]{0:T(128)} %ray_hbm.1, s32[64]{0:T(128)} %cell_hbm.1, s32[16]{0:T(128)} %survey_ref.11, f32[8,64,256]{2,1,0:T(8,128)} %prior_ref.5, ...), custom_call_target="tpu_custom_call" | custom-call | tf_op jit(solution)/shard_map/pallas_call | solution.py:228
  3.7 0.5 collective-permute-start
  4.2 0.1 collective-permute-start.1
  4.3 0.7 collective-permute-start.2
  5.0 0.4 collective-permute-done
  5.4 0.4 collective-permute-done.1.chip_ref
  5.8 15.4 %all_to_all.30 = f16[8,64,128]{2,1,0:T(8,128)(2,1)S(1)} all-to-all(f16[8,64,128]{2,1,0:T(8,128)(2,1)S(1)} %multiply_convert_fusion.2), channel_id=1, replica_groups={{0,2,4,6,8,10,12,14},{1,3,5,7,9,11,13,15},{16,18,20,22,24,26,28,30},{17..., dimensions={0} | all-to-all | bytes 262144 | tf_op jit(solution)/shard_map/all_to_all | solution.py:252
  21.1 0.0 collective-permute-done.2.halo_ref.link_ref
  21.2 9.9 %all_to_all.31.residual_ref = bf16[8,64,128]{2,1,0:T(8,128)(2,1)S(1)} all-to-all(bf16[8,64,128]{2,1,0:T(8,128)(2,1)S(1)} %bitcast.9), channel_id=1, replica_groups={{0,2,4,6,8,10,12,14},{1,3,5,7,9,11,13,15},{16,18,20,22,24,26,28,30},{17..., dimensions={0} | all-to-all | bytes 262144 | tf_op jit(solution)/shard_map/all_to_all | solution.py:252
  31.1 0.9 %shard_map.98 = (f32[8,32,256]{2,1,0:T(8,128)S(1)}, f32[8,32,256]{2,1,0:T(8,128)S(1)}) custom-call(s32[16]{0:T(128)S(1)} %copy-done.2, bf16[8,64,128]{2,1,0:T(8,128)(2,1)S(1)} %all_to_all.31.residual_ref, bf16[16,128,256]{2,1,0:T(8,128)(2,1)S(1)} %get-tuple-element.46.dense_ref, f32[8,64,256]{2,1,0:T(8,128)S(1)} %copy-done, f32[8,64,256]{2,1,0:T(8,128)S(1)} %copy-done, ...), custom_call_target="tpu_custom_call" | custom-call | tf_op jit(solution)/shard_map/pallas_call | solution.py:284
  32.0 0.4 collective-permute-done.3.residual_ref
  32.4 1.3 %shard_map.99 = (f32[8,64,256]{2,1,0:T(8,128)S(1)}, bf16[8,64,256]{2,1,0:T(8,128)(2,1)S(1)}, f32[8,64,128]{2,1,0:T(8,128)S(1)}, f32[8,64,128]{2,1,0:T(8,128)S(1)}) custom-call(s32[16]{0:T(128)S(1)} %copy-done.2, bf16[8,64,128]{2,1,0:T(8,128)(2,1)S(1)} %collective-permute-done.3.residual_ref, bf16[16,128,256]{2,1,0:T(8,128)(2,1)S(1)} %get-tuple-element.46.dense_ref, ...), custom_call_target="tpu_custom_call" | custom-call | tf_op jit(solution)/shard_map/pallas_call | solution.py:293
  33.8 0.2 collective-permute-start.4
  34.0 0.4 collective-permute-start.5
  34.3 0.7 collective-permute-start.6
  35.0 0.4 collective-permute-done.4
  35.4 0.4 collective-permute-done.5.chip_ref
  35.8 10.9 %all_to_all.32 = f16[8,64,128]{2,1,0:T(8,128)(2,1)S(1)} all-to-all(f16[8,64,128]{2,1,0:T(8,128)(2,1)S(1)} %multiply_convert_fusion.1), channel_id=1, replica_groups={{0,2,4,6,8,10,12,14},{1,3,5,7,9,11,13,15},{16,18,20,22,24,26,28,30},{17..., dimensions={0} | all-to-all | bytes 262144 | tf_op jit(solution)/shard_map/all_to_all | solution.py:252
  46.8 9.8 %all_to_all.33.residual_ref = bf16[8,64,128]{2,1,0:T(8,128)(2,1)S(1)} all-to-all(bf16[8,64,128]{2,1,0:T(8,128)(2,1)S(1)} %bitcast.10), channel_id=1, replica_groups={{0,2,4,6,8,10,12,14},{1,3,5,7,9,11,13,15},{16,18,20,22,24,26,28,30},{17..., dimensions={0} | all-to-all | bytes 262144 | tf_op jit(solution)/shard_map/all_to_all | solution.py:252
  56.6 0.9 %shard_map.102 = (f32[8,32,256]{2,1,0:T(8,128)S(1)}, f32[8,32,256]{2,1,0:T(8,128)S(1)}) custom-call(s32[16]{0:T(128)S(1)} %copy-done.2, bf16[8,64,128]{2,1,0:T(8,128)(2,1)S(1)} %all_to_all.33.residual_ref, bf16[16,128,256]{2,1,0:T(8,128)(2,1)S(1)} %get-tuple-element.46.dense_ref, f32[8,64,256]{2,1,0:T(8,128)S(1)} %get-tuple-element.58.members_ref, ...), custom_call_target="tpu_custom_call" | custom-call | tf_op jit(solution)/shard_map/pallas_call | solution.py:284
  57.5 0.4 collective-permute-done.7.residual_ref
  57.9 1.3 %shard_map.103 = (f32[8,64,256]{2,1,0:T(8,128)S(1)}, bf16[8,64,256]{2,1,0:T(8,128)(2,1)S(1)}, f32[8,64,128]{2,1,0:T(8,128)S(1)}, f32[8,64,128]{2,1,0:T(8,128)S(1)}) custom-call(s32[16]{0:T(128)S(1)} %copy-done.2, bf16[8,64,128]{2,1,0:T(8,128)(2,1)S(1)} %collective-permute-done.7.residual_ref, bf16[16,128,256]{2,1,0:T(8,128)(2,1)S(1)} %get-tuple-element.46.dense_ref, ...), custom_call_target="tpu_custom_call" | custom-call | tf_op jit(solution)/shard_map/pallas_call | solution.py:293
  59.3 0.2 collective-permute-start.8
  59.5 0.4 collective-permute-start.9
  59.8 0.7 collective-permute-start.10
  60.5 0.4 collective-permute-done.8
  60.9 0.4 collective-permute-done.9.chip_ref
  61.3 10.9 %all_to_all.34 = f16[8,64,128]{2,1,0:T(8,128)(2,1)S(1)} all-to-all(f16[8,64,128]{2,1,0:T(8,128)(2,1)S(1)} %multiply_convert_fusion), channel_id=1, replica_groups={{0,2,4,6,8,10,12,14},{1,3,5,7,9,11,13,15},{16,18,20,22,24,26,28,30},{17..., dimensions={0} | all-to-all | bytes 262144 | tf_op jit(solution)/shard_map/all_to_all | solution.py:252
  72.3 9.8 %all_to_all.35.residual_ref = bf16[8,64,128]{2,1,0:T(8,128)(2,1)S(1)} all-to-all(bf16[8,64,128]{2,1,0:T(8,128)(2,1)S(1)} %bitcast.11), channel_id=1, replica_groups={{0,2,4,6,8,10,12,14},{1,3,5,7,9,11,13,15},{16,18,20,22,24,26,28,30},{17..., dimensions={0} | all-to-all | bytes 262144 | tf_op jit(solution)/shard_map/all_to_all | solution.py:252
  82.1 0.9 %shard_map.106 = (f32[8,32,256]{2,1,0:T(8,128)S(1)}, f32[8,32,256]{2,1,0:T(8,128)S(1)}) custom-call(s32[16]{0:T(128)S(1)} %copy-done.2, bf16[8,64,128]{2,1,0:T(8,128)(2,1)S(1)} %all_to_all.35.residual_ref, bf16[16,128,256]{2,1,0:T(8,128)(2,1)S(1)} %get-tuple-element.46.dense_ref, f32[8,64,256]{2,1,0:T(8,128)S(1)} %get-tuple-element.70.members_ref, ...), custom_call_target="tpu_custom_call" | custom-call | tf_op jit(solution)/shard_map/pallas_call | solution.py:284
  83.0 0.4 collective-permute-done.11.residual_ref
  83.4 1.7 %shard_map.107 = (f32[8,64,256]{2,1,0:T(8,128)}, bf16[8,64,256]{2,1,0:T(8,128)(2,1)}) custom-call(s32[16]{0:T(128)S(1)} %copy-done.2, bf16[8,64,128]{2,1,0:T(8,128)(2,1)S(1)} %collective-permute-done.11.residual_ref, bf16[16,128,256]{2,1,0:T(8,128)(2,1)S(1)} %get-tuple-element.46.dense_ref, f32[8,32,256]{2,1,0:T(8,128)S(1)} %get-tuple-element.72.upper_ref, ...), custom_call_target="tpu_custom_call" | custom-call | tf_op jit(solution)/shard_map/pallas_call | solution.py:293
  (28 shorter events, 0.3 us)
Async XLA Ops:
  0.6 20.5 %copy-start.1 = (f32[1,64,128]{2,1,0:T(8,128)S(1)}, f32[1,64,128]{2,1,0:T(8,128)}, u32[]{:S(2)}) copy-start(f32[1,64,128]{2,1,0:T(8,128)} %observed_ref.8) | copy-start | bytes 98308
  0.6 20.6 %copy-start.3 = (f32[1,128]{1,0:T(1,128)S(1)}, f32[1,128]{1,0:T(1,128)}, u32[]{:S(2)}) copy-start(f32[1,128]{1,0:T(1,128)} %noise_ref.5) | copy-start | bytes 1540
  1.3 29.8 %copy-start = (f32[8,64,256]{2,1,0:T(8,128)S(1)}, f32[8,64,256]{2,1,0:T(8,128)}, u32[]{:S(2)}) copy-start(f32[8,64,256]{2,1,0:T(8,128)} %prior_ref.5) | copy-start | bytes 1572868
  1.3 29.8 %copy-start.2 = (s32[16]{0:T(128)S(1)}, s32[16]{0:T(128)}, u32[]{:S(2)}) copy-start(s32[16]{0:T(128)} %survey_ref.11) | copy-start | bytes 196
  3.7 1.7 %collective-permute-start = (f32[8,64,128]{2,1,0:T(8,128)S(1)}, f32[8,64,128]{2,1,0:T(8,128)S(1)}, u32[]{:S(2)}, u32[]{:S(2)}) collective-permute-start(f32[8,64,128]{2,1,0:T(8,128)S(1)} %get-tuple-element.39), channel_id=1, source_target_pairs={{0,1},{1,0},{2,3},{3,2},{4,5},{5,4},{6,7},{7,6},{8,9},{9,8},{10,11... | collective-permute-start | bytes 786440 | tf_op jit(solution)/shard_map/ppermute | solution.py:258
  4.2 1.5 %collective-permute-start.1 = (bf16[8,64,256]{2,1,0:T(8,128)(2,1)S(1)}, bf16[8,64,256]{2,1,0:T(8,128)(2,1)S(1)}, u32[]{:S(2)}, u32[]{:S(2)}) collective-permute-start(bf16[8,64,256]{2,1,0:T(8,128)(2,1)S(1)} %get-tuple-element.40), channel_id=1, source_target_pairs={{0,1},{1,0},{2,3},{3,2},{4,5},{5,4},{6,7},{7,6},{8,9},{9,8},{10,11... | collective-permute-start | bytes 786440 | tf_op jit(solution)/shard_map/ppermute | solution.py:259
  4.3 16.9 %collective-permute-start.2 = (bf16[8,64,256]{2,1,0:T(8,128)(2,1)S(1)}, bf16[8,64,256]{2,1,0:T(8,128)(2,1)S(1)}, u32[]{:S(2)}, u32[]{:S(2)}) collective-permute-start(bf16[8,64,256]{2,1,0:T(8,128)(2,1)S(1)} %get-tuple-element.40), channel_id=1, source_target_pairs={{1,2},{2,1},{3,4},{4,3},{5,6},{6,5},{7,8},{8,7},{9,10},{10,9},{11,... | collective-permute-start | bytes 786440 | tf_op jit(solution)/shard_map/ppermute | solution.py:262
  31.1 1.3 %collective-permute-start.3 = (bf16[8,64,128]{2,1,0:T(8,128)(2,1)S(1)}, bf16[8,64,128]{2,1,0:T(8,128)(2,1)S(1)}, u32[]{:S(2)}, u32[]{:S(2)}) collective-permute-start(bf16[8,64,128]{2,1,0:T(8,128)(2,1)S(1)} %all_to_all.31.residual_ref), channel_id=1, source_target_pairs={{0,1},{1,0},{2,3},{3,2},{4,5},{5,4},{6,7},{7,6},{8,9},{9,8},{10,11... | collective-permute-start | bytes 393224 | tf_op jit(solution)/shard_map/ppermute | solution.py:283
  33.8 1.6 %collective-permute-start.4 = (f32[8,64,128]{2,1,0:T(8,128)S(1)}, f32[8,64,128]{2,1,0:T(8,128)S(1)}, u32[]{:S(2)}, u32[]{:S(2)}) collective-permute-start(f32[8,64,128]{2,1,0:T(8,128)S(1)} %get-tuple-element.51), channel_id=1, source_target_pairs={{0,1},{1,0},{2,3},{3,2},{4,5},{5,4},{6,7},{7,6},{8,9},{9,8},{10,11... | collective-permute-start | bytes 786440 | tf_op jit(solution)/shard_map/ppermute | solution.py:258
  34.0 1.8 %collective-permute-start.5 = (bf16[8,64,256]{2,1,0:T(8,128)(2,1)S(1)}, bf16[8,64,256]{2,1,0:T(8,128)(2,1)S(1)}, u32[]{:S(2)}, u32[]{:S(2)}) collective-permute-start(bf16[8,64,256]{2,1,0:T(8,128)(2,1)S(1)} %get-tuple-element.52), channel_id=1, source_target_pairs={{0,1},{1,0},{2,3},{3,2},{4,5},{5,4},{6,7},{7,6},{8,9},{9,8},{10,11... | collective-permute-start | bytes 786440 | tf_op jit(solution)/shard_map/ppermute | solution.py:259
  34.3 12.3 %collective-permute-start.6 = (bf16[8,64,256]{2,1,0:T(8,128)(2,1)S(1)}, bf16[8,64,256]{2,1,0:T(8,128)(2,1)S(1)}, u32[]{:S(2)}, u32[]{:S(2)}) collective-permute-start(bf16[8,64,256]{2,1,0:T(8,128)(2,1)S(1)} %get-tuple-element.52), channel_id=1, source_target_pairs={{1,2},{2,1},{3,4},{4,3},{5,6},{6,5},{7,8},{8,7},{9,10},{10,9},{11,... | collective-permute-start | bytes 786440 | tf_op jit(solution)/shard_map/ppermute | solution.py:262
  56.6 1.3 %collective-permute-start.7 = (bf16[8,64,128]{2,1,0:T(8,128)(2,1)S(1)}, bf16[8,64,128]{2,1,0:T(8,128)(2,1)S(1)}, u32[]{:S(2)}, u32[]{:S(2)}) collective-permute-start(bf16[8,64,128]{2,1,0:T(8,128)(2,1)S(1)} %all_to_all.33.residual_ref), channel_id=1, source_target_pairs={{0,1},{1,0},{2,3},{3,2},{4,5},{5,4},{6,7},{7,6},{8,9},{9,8},{10,11... | collective-permute-start | bytes 393224 | tf_op jit(solution)/shard_map/ppermute | solution.py:283
  59.3 1.6 %collective-permute-start.8 = (f32[8,64,128]{2,1,0:T(8,128)S(1)}, f32[8,64,128]{2,1,0:T(8,128)S(1)}, u32[]{:S(2)}, u32[]{:S(2)}) collective-permute-start(f32[8,64,128]{2,1,0:T(8,128)S(1)} %get-tuple-element.63), channel_id=1, source_target_pairs={{0,1},{1,0},{2,3},{3,2},{4,5},{5,4},{6,7},{7,6},{8,9},{9,8},{10,11... | collective-permute-start | bytes 786440 | tf_op jit(solution)/shard_map/ppermute | solution.py:258
  59.5 1.8 %collective-permute-start.9 = (bf16[8,64,256]{2,1,0:T(8,128)(2,1)S(1)}, bf16[8,64,256]{2,1,0:T(8,128)(2,1)S(1)}, u32[]{:S(2)}, u32[]{:S(2)}) collective-permute-start(bf16[8,64,256]{2,1,0:T(8,128)(2,1)S(1)} %get-tuple-element.64), channel_id=1, source_target_pairs={{0,1},{1,0},{2,3},{3,2},{4,5},{5,4},{6,7},{7,6},{8,9},{9,8},{10,11... | collective-permute-start | bytes 786440 | tf_op jit(solution)/shard_map/ppermute | solution.py:259
  59.8 12.3 %collective-permute-start.10 = (bf16[8,64,256]{2,1,0:T(8,128)(2,1)S(1)}, bf16[8,64,256]{2,1,0:T(8,128)(2,1)S(1)}, u32[]{:S(2)}, u32[]{:S(2)}) collective-permute-start(bf16[8,64,256]{2,1,0:T(8,128)(2,1)S(1)} %get-tuple-element.64), channel_id=1, source_target_pairs={{1,2},{2,1},{3,4},{4,3},{5,6},{6,5},{7,8},{8,7},{9,10},{10,9},{11,... | collective-permute-start | bytes 786440 | tf_op jit(solution)/shard_map/ppermute | solution.py:262
  82.1 1.3 %collective-permute-start.11 = (bf16[8,64,128]{2,1,0:T(8,128)(2,1)S(1)}, bf16[8,64,128]{2,1,0:T(8,128)(2,1)S(1)}, u32[]{:S(2)}, u32[]{:S(2)}) collective-permute-start(bf16[8,64,128]{2,1,0:T(8,128)(2,1)S(1)} %all_to_all.35.residual_ref), channel_id=1, source_target_pairs={{0,1},{1,0},{2,3},{3,2},{4,5},{5,4},{6,7},{7,6},{8,9},{9,8},{10,11... | collective-permute-start | bytes 393224 | tf_op jit(solution)/shard_map/ppermute | solution.py:283

commit v2 on v1

--- a/solution.py
+++ b/solution.py
@@ -17,7 +17,7 @@
 
 SENT_SCALE = 1.0 / 32.0
 
-CHUNK = 8
+CHUNK = 16
 VMEM_BYTES = 24 * 1024 * 1024
 SETUP_VMEM_BYTES = 60 * 1024 * 1024
 

time: 85.6 us -> 85.6 us (level)
  no operation moved by 1% of the time
where the time goes in v2:
time: 85.6 us; the launch traced here: 85.2 us
  blocking collectives  66.7 us (78%)
  Pallas kernels  9.57 us (11%)
  starting transfers between devices  3.75 us (4%)
  waiting for transfers between devices  3.47 us (4%)
  between operations  1.49 us (2%)
    all_to_all x6, blocking collectives, exchange(): lax.all_to_all(array, 'cell', split_axis=0, concat_axis=0, axis_index_gro...  66.7 us
    pallas_call x3, Pallas kernels, shards(): pl.pallas_call(functools.partial(last_kernel if last else step_kernel, or...  4.32 us
    pallas_call x3, Pallas kernels, shards(): pl.pallas_call(functools.partial(gradient_kernel, order), out_shape=(part...  2.78 us
    pallas_call x1, Pallas kernels, shards(): pl.pallas_call(functools.partial(setup_kernel, order), out_shape=(bf16(ra...  2.38 us
    ppermute x3, starting transfers between devices, shards(): link_halo = lax.ppermute(half, 'cell', link_pairs)  2 us
  transfers between devices with their start and end apart: 12, of which 9 were waited for; matrix products, arithmetic and copies ran while one was open for 0% of the time, Pallas kernels for 3%

profile of v2, /device:TPU:0, one launch (start us, length us, event | category | flops | bytes accessed | tf_op | source)
XLA Modules:
  0.0 85.2 jit_solution(10869181456395824080)
XLA Ops:
  1.3 2.4 %shard_map.95 = (bf16[16,128,256]{2,1,0:T(8,128)(2,1)S(1)}, bf16[8,64,256]{2,1,0:T(8,128)(2,1)S(1)}, f32[8,64,128]{2,1,0:T(8,128)S(1)}, f32[8,64,128]{2,1,0:T(8,128)S(1)}) custom-call(s32[1]{0:T(128)S(6)} %copy.10.count_ref, s32[64]{0:T(128)} %ray_hbm.1, s32[64]{0:T(128)} %cell_hbm.1, s32[16]{0:T(128)} %survey_ref.11, f32[8,64,256]{2,1,0:T(8,128)} %prior_ref.5, ...), custom_call_target="tpu_custom_call" | custom-call | tf_op jit(solution)/shard_map/pallas_call | solution.py:228
  3.7 0.5 collective-permute-start
  4.2 0.1 collective-permute-start.1
  4.3 0.7 collective-permute-start.2
  5.0 0.4 collective-permute-done
  5.4 0.4 collective-permute-done.1.chip_ref
  5.8 15.4 %all_to_all.30 = f16[8,64,128]{2,1,0:T(8,128)(2,1)S(1)} all-to-all(f16[8,64,128]{2,1,0:T(8,128)(2,1)S(1)} %multiply_convert_fusion.2), channel_id=1, replica_groups={{0,2,4,6,8,10,12,14},{1,3,5,7,9,11,13,15},{16,18,20,22,24,26,28,30},{17..., dimensions={0} | all-to-all | bytes 262144 | tf_op jit(solution)/shard_map/all_to_all | solution.py:252
  21.3 9.9 %all_to_all.31.residual_ref = bf16[8,64,128]{2,1,0:T(8,128)(2,1)S(1)} all-to-all(bf16[8,64,128]{2,1,0:T(8,128)(2,1)S(1)} %bitcast.9), channel_id=1, replica_groups={{0,2,4,6,8,10,12,14},{1,3,5,7,9,11,13,15},{16,18,20,22,24,26,28,30},{17..., dimensions={0} | all-to-all | bytes 262144 | tf_op jit(solution)/shard_map/all_to_all | solution.py:252
  31.1 0.0 collective-permute-start.3
  31.1 0.9 %shard_map.98 = (f32[8,32,256]{2,1,0:T(8,128)S(1)}, f32[8,32,256]{2,1,0:T(8,128)S(1)}) custom-call(s32[16]{0:T(128)S(1)} %copy-done.2, bf16[8,64,128]{2,1,0:T(8,128)(2,1)S(1)} %all_to_all.31.residual_ref, bf16[16,128,256]{2,1,0:T(8,128)(2,1)S(1)} %get-tuple-element.46.dense_ref, f32[8,64,256]{2,1,0:T(8,128)S(1)} %copy-done, f32[8,64,256]{2,1,0:T(8,128)S(1)} %copy-done, ...), custom_call_target="tpu_custom_call" | custom-call | tf_op jit(solution)/shard_map/pallas_call | solution.py:284
  32.1 0.4 collective-permute-done.3.residual_ref
  32.5 1.3 %shard_map.99 = (f32[8,64,256]{2,1,0:T(8,128)S(1)}, bf16[8,64,256]{2,1,0:T(8,128)(2,1)S(1)}, f32[8,64,128]{2,1,0:T(8,128)S(1)}, f32[8,64,128]{2,1,0:T(8,128)S(1)}) custom-call(s32[16]{0:T(128)S(1)} %copy-done.2, bf16[8,64,128]{2,1,0:T(8,128)(2,1)S(1)} %collective-permute-done.3.residual_ref, bf16[16,128,256]{2,1,0:T(8,128)(2,1)S(1)} %get-tuple-element.46.dense_ref, ...), custom_call_target="tpu_custom_call" | custom-call | tf_op jit(solution)/shard_map/pallas_call | solution.py:293
  33.8 0.2 collective-permute-start.4
  34.0 0.4 collective-permute-start.5
  34.4 0.7 collective-permute-start.6
  35.0 0.4 collective-permute-done.4
  35.4 0.4 collective-permute-done.5.chip_ref
  35.8 10.9 %all_to_all.32 = f16[8,64,128]{2,1,0:T(8,128)(2,1)S(1)} all-to-all(f16[8,64,128]{2,1,0:T(8,128)(2,1)S(1)} %multiply_convert_fusion.1), channel_id=1, replica_groups={{0,2,4,6,8,10,12,14},{1,3,5,7,9,11,13,15},{16,18,20,22,24,26,28,30},{17..., dimensions={0} | all-to-all | bytes 262144 | tf_op jit(solution)/shard_map/all_to_all | solution.py:252
  46.8 9.8 %all_to_all.33.residual_ref = bf16[8,64,128]{2,1,0:T(8,128)(2,1)S(1)} all-to-all(bf16[8,64,128]{2,1,0:T(8,128)(2,1)S(1)} %bitcast.10), channel_id=1, replica_groups={{0,2,4,6,8,10,12,14},{1,3,5,7,9,11,13,15},{16,18,20,22,24,26,28,30},{17..., dimensions={0} | all-to-all | bytes 262144 | tf_op jit(solution)/shard_map/all_to_all | solution.py:252
  56.6 0.9 %shard_map.102 = (f32[8,32,256]{2,1,0:T(8,128)S(1)}, f32[8,32,256]{2,1,0:T(8,128)S(1)}) custom-call(s32[16]{0:T(128)S(1)} %copy-done.2, bf16[8,64,128]{2,1,0:T(8,128)(2,1)S(1)} %all_to_all.33.residual_ref, bf16[16,128,256]{2,1,0:T(8,128)(2,1)S(1)} %get-tuple-element.46.dense_ref, f32[8,64,256]{2,1,0:T(8,128)S(1)} %get-tuple-element.58.members_ref, ...), custom_call_target="tpu_custom_call" | custom-call | tf_op jit(solution)/shard_map/pallas_call | solution.py:284
  57.6 0.4 collective-permute-done.7.residual_ref
  58.0 1.3 %shard_map.103 = (f32[8,64,256]{2,1,0:T(8,128)S(1)}, bf16[8,64,256]{2,1,0:T(8,128)(2,1)S(1)}, f32[8,64,128]{2,1,0:T(8,128)S(1)}, f32[8,64,128]{2,1,0:T(8,128)S(1)}) custom-call(s32[16]{0:T(128)S(1)} %copy-done.2, bf16[8,64,128]{2,1,0:T(8,128)(2,1)S(1)} %collective-permute-done.7.residual_ref, bf16[16,128,256]{2,1,0:T(8,128)(2,1)S(1)} %get-tuple-element.46.dense_ref, ...), custom_call_target="tpu_custom_call" | custom-call | tf_op jit(solution)/shard_map/pallas_call | solution.py:293
  59.3 0.2 collective-permute-start.8
  59.5 0.4 collective-permute-start.9
  59.9 0.7 collective-permute-start.10
  60.5 0.4 collective-permute-done.8
  60.9 0.4 collective-permute-done.9.chip_ref
  61.3 10.9 %all_to_all.34 = f16[8,64,128]{2,1,0:T(8,128)(2,1)S(1)} all-to-all(f16[8,64,128]{2,1,0:T(8,128)(2,1)S(1)} %multiply_convert_fusion), channel_id=1, replica_groups={{0,2,4,6,8,10,12,14},{1,3,5,7,9,11,13,15},{16,18,20,22,24,26,28,30},{17..., dimensions={0} | all-to-all | bytes 262144 | tf_op jit(solution)/shard_map/all_to_all | solution.py:252
  72.3 9.8 %all_to_all.35.residual_ref = bf16[8,64,128]{2,1,0:T(8,128)(2,1)S(1)} all-to-all(bf16[8,64,128]{2,1,0:T(8,128)(2,1)S(1)} %bitcast.11), channel_id=1, replica_groups={{0,2,4,6,8,10,12,14},{1,3,5,7,9,11,13,15},{16,18,20,22,24,26,28,30},{17..., dimensions={0} | all-to-all | bytes 262144 | tf_op jit(solution)/shard_map/all_to_all | solution.py:252
  82.1 0.9 %shard_map.106 = (f32[8,32,256]{2,1,0:T(8,128)S(1)}, f32[8,32,256]{2,1,0:T(8,128)S(1)}) custom-call(s32[16]{0:T(128)S(1)} %copy-done.2, bf16[8,64,128]{2,1,0:T(8,128)(2,1)S(1)} %all_to_all.35.residual_ref, bf16[16,128,256]{2,1,0:T(8,128)(2,1)S(1)} %get-tuple-element.46.dense_ref, f32[8,64,256]{2,1,0:T(8,128)S(1)} %get-tuple-element.70.members_ref, ...), custom_call_target="tpu_custom_call" | custom-call | tf_op jit(solution)/shard_map/pallas_call | solution.py:284
  83.1 0.4 collective-permute-done.11.residual_ref
  83.5 1.7 %shard_map.107 = (f32[8,64,256]{2,1,0:T(8,128)}, bf16[8,64,256]{2,1,0:T(8,128)(2,1)}) custom-call(s32[16]{0:T(128)S(1)} %copy-done.2, bf16[8,64,128]{2,1,0:T(8,128)(2,1)S(1)} %collective-permute-done.11.residual_ref, bf16[16,128,256]{2,1,0:T(8,128)(2,1)S(1)} %get-tuple-element.46.dense_ref, f32[8,32,256]{2,1,0:T(8,128)S(1)} %get-tuple-element.72.upper_ref, ...), custom_call_target="tpu_custom_call" | custom-call | tf_op jit(solution)/shard_map/pallas_call | solution.py:293
  (28 shorter events, 0.3 us)
Async XLA Ops:
  0.6 20.6 %copy-start.1 = (f32[1,64,128]{2,1,0:T(8,128)S(1)}, f32[1,64,128]{2,1,0:T(8,128)}, u32[]{:S(2)}) copy-start(f32[1,64,128]{2,1,0:T(8,128)} %observed_ref.8) | copy-start | bytes 98308
  0.6 20.6 %copy-start.3 = (f32[1,128]{1,0:T(1,128)S(1)}, f32[1,128]{1,0:T(1,128)}, u32[]{:S(2)}) copy-start(f32[1,128]{1,0:T(1,128)} %noise_ref.5) | copy-start | bytes 1540
  1.3 29.8 %copy-start = (f32[8,64,256]{2,1,0:T(8,128)S(1)}, f32[8,64,256]{2,1,0:T(8,128)}, u32[]{:S(2)}) copy-start(f32[8,64,256]{2,1,0:T(8,128)} %prior_ref.5) | copy-start | bytes 1572868
  1.3 29.8 %copy-start.2 = (s32[16]{0:T(128)S(1)}, s32[16]{0:T(128)}, u32[]{:S(2)}) copy-start(s32[16]{0:T(128)} %survey_ref.11) | copy-start | bytes 196
  3.7 1.7 %collective-permute-start = (f32[8,64,128]{2,1,0:T(8,128)S(1)}, f32[8,64,128]{2,1,0:T(8,128)S(1)}, u32[]{:S(2)}, u32[]{:S(2)}) collective-permute-start(f32[8,64,128]{2,1,0:T(8,128)S(1)} %get-tuple-element.39), channel_id=1, source_target_pairs={{0,1},{1,0},{2,3},{3,2},{4,5},{5,4},{6,7},{7,6},{8,9},{9,8},{10,11... | collective-permute-start | bytes 786440 | tf_op jit(solution)/shard_map/ppermute | solution.py:258
  4.2 1.5 %collective-permute-start.1 = (bf16[8,64,256]{2,1,0:T(8,128)(2,1)S(1)}, bf16[8,64,256]{2,1,0:T(8,128)(2,1)S(1)}, u32[]{:S(2)}, u32[]{:S(2)}) collective-permute-start(bf16[8,64,256]{2,1,0:T(8,128)(2,1)S(1)} %get-tuple-element.40), channel_id=1, source_target_pairs={{0,1},{1,0},{2,3},{3,2},{4,5},{5,4},{6,7},{7,6},{8,9},{9,8},{10,11... | collective-permute-start | bytes 786440 | tf_op jit(solution)/shard_map/ppermute | solution.py:259
  4.3 16.9 %collective-permute-start.2 = (bf16[8,64,256]{2,1,0:T(8,128)(2,1)S(1)}, bf16[8,64,256]{2,1,0:T(8,128)(2,1)S(1)}, u32[]{:S(2)}, u32[]{:S(2)}) collective-permute-start(bf16[8,64,256]{2,1,0:T(8,128)(2,1)S(1)} %get-tuple-element.40), channel_id=1, source_target_pairs={{1,2},{2,1},{3,4},{4,3},{5,6},{6,5},{7,8},{8,7},{9,10},{10,9},{11,... | collective-permute-start | bytes 786440 | tf_op jit(solution)/shard_map/ppermute | solution.py:262
  31.1 1.3 %collective-permute-start.3 = (bf16[8,64,128]{2,1,0:T(8,128)(2,1)S(1)}, bf16[8,64,128]{2,1,0:T(8,128)(2,1)S(1)}, u32[]{:S(2)}, u32[]{:S(2)}) collective-permute-start(bf16[8,64,128]{2,1,0:T(8,128)(2,1)S(1)} %all_to_all.31.residual_ref), channel_id=1, source_target_pairs={{0,1},{1,0},{2,3},{3,2},{4,5},{5,4},{6,7},{7,6},{8,9},{9,8},{10,11... | collective-permute-start | bytes 393224 | tf_op jit(solution)/shard_map/ppermute | solution.py:283
  33.8 1.6 %collective-permute-start.4 = (f32[8,64,128]{2,1,0:T(8,128)S(1)}, f32[8,64,128]{2,1,0:T(8,128)S(1)}, u32[]{:S(2)}, u32[]{:S(2)}) collective-permute-start(f32[8,64,128]{2,1,0:T(8,128)S(1)} %get-tuple-element.51), channel_id=1, source_target_pairs={{0,1},{1,0},{2,3},{3,2},{4,5},{5,4},{6,7},{7,6},{8,9},{9,8},{10,11... | collective-permute-start | bytes 786440 | tf_op jit(solution)/shard_map/ppermute | solution.py:258
  34.0 1.8 %collective-permute-start.5 = (bf16[8,64,256]{2,1,0:T(8,128)(2,1)S(1)}, bf16[8,64,256]{2,1,0:T(8,128)(2,1)S(1)}, u32[]{:S(2)}, u32[]{:S(2)}) collective-permute-start(bf16[8,64,256]{2,1,0:T(8,128)(2,1)S(1)} %get-tuple-element.52), channel_id=1, source_target_pairs={{0,1},{1,0},{2,3},{3,2},{4,5},{5,4},{6,7},{7,6},{8,9},{9,8},{10,11... | collective-permute-start | bytes 786440 | tf_op jit(solution)/shard_map/ppermute | solution.py:259
  34.4 12.3 %collective-permute-start.6 = (bf16[8,64,256]{2,1,0:T(8,128)(2,1)S(1)}, bf16[8,64,256]{2,1,0:T(8,128)(2,1)S(1)}, u32[]{:S(2)}, u32[]{:S(2)}) collective-permute-start(bf16[8,64,256]{2,1,0:T(8,128)(2,1)S(1)} %get-tuple-element.52), channel_id=1, source_target_pairs={{1,2},{2,1},{3,4},{4,3},{5,6},{6,5},{7,8},{8,7},{9,10},{10,9},{11,... | collective-permute-start | bytes 786440 | tf_op jit(solution)/shard_map/ppermute | solution.py:262
  56.6 1.3 %collective-permute-start.7 = (bf16[8,64,128]{2,1,0:T(8,128)(2,1)S(1)}, bf16[8,64,128]{2,1,0:T(8,128)(2,1)S(1)}, u32[]{:S(2)}, u32[]{:S(2)}) collective-permute-start(bf16[8,64,128]{2,1,0:T(8,128)(2,1)S(1)} %all_to_all.33.residual_ref), channel_id=1, source_target_pairs={{0,1},{1,0},{2,3},{3,2},{4,5},{5,4},{6,7},{7,6},{8,9},{9,8},{10,11... | collective-permute-start | bytes 393224 | tf_op jit(solution)/shard_map/ppermute | solution.py:283
  59.3 1.6 %collective-permute-start.8 = (f32[8,64,128]{2,1,0:T(8,128)S(1)}, f32[8,64,128]{2,1,0:T(8,128)S(1)}, u32[]{:S(2)}, u32[]{:S(2)}) collective-permute-start(f32[8,64,128]{2,1,0:T(8,128)S(1)} %get-tuple-element.63), channel_id=1, source_target_pairs={{0,1},{1,0},{2,3},{3,2},{4,5},{5,4},{6,7},{7,6},{8,9},{9,8},{10,11... | collective-permute-start | bytes 786440 | tf_op jit(solution)/shard_map/ppermute | solution.py:258
  59.5 1.8 %collective-permute-start.9 = (bf16[8,64,256]{2,1,0:T(8,128)(2,1)S(1)}, bf16[8,64,256]{2,1,0:T(8,128)(2,1)S(1)}, u32[]{:S(2)}, u32[]{:S(2)}) collective-permute-start(bf16[8,64,256]{2,1,0:T(8,128)(2,1)S(1)} %get-tuple-element.64), channel_id=1, source_target_pairs={{0,1},{1,0},{2,3},{3,2},{4,5},{5,4},{6,7},{7,6},{8,9},{9,8},{10,11... | collective-permute-start | bytes 786440 | tf_op jit(solution)/shard_map/ppermute | solution.py:259
  59.9 12.4 %collective-permute-start.10 = (bf16[8,64,256]{2,1,0:T(8,128)(2,1)S(1)}, bf16[8,64,256]{2,1,0:T(8,128)(2,1)S(1)}, u32[]{:S(2)}, u32[]{:S(2)}) collective-permute-start(bf16[8,64,256]{2,1,0:T(8,128)(2,1)S(1)} %get-tuple-element.64), channel_id=1, source_target_pairs={{1,2},{2,1},{3,4},{4,3},{5,6},{6,5},{7,8},{8,7},{9,10},{10,9},{11,... | collective-permute-start | bytes 786440 | tf_op jit(solution)/shard_map/ppermute | solution.py:262
  82.1 1.3 %collective-permute-start.11 = (bf16[8,64,128]{2,1,0:T(8,128)(2,1)S(1)}, bf16[8,64,128]{2,1,0:T(8,128)(2,1)S(1)}, u32[]{:S(2)}, u32[]{:S(2)}) collective-permute-start(bf16[8,64,128]{2,1,0:T(8,128)(2,1)S(1)} %all_to_all.35.residual_ref), channel_id=1, source_target_pairs={{0,1},{1,0},{2,3},{3,2},{4,5},{5,4},{6,7},{7,6},{8,9},{9,8},{10,11... | collective-permute-start | bytes 393224 | tf_op jit(solution)/shard_map/ppermute | solution.py:283
